TPU v7x, 32 devices: a whole 2x2x4 slice. The times are simulated.
32 devices in a mesh: seq: 8 (over z, x), head: 4 (over y, core).
Axes of the slice: x: 2, y: 2, z: 4, core: 2. Of those that a mesh axis runs over, the one named last changes fastest.
Arguments:
- queries: bfloat16 [8192, 4096], P(('seq', 'head')), may hold values from -8 to 8
- key_rows: bfloat16 [8192, 2048], P(('seq', 'head')), may hold values from -8 to 8
- value_rows: bfloat16 [8192, 2048], P(('seq', 'head')), may hold values from -6 to 6
Outputs:
- attended: bfloat16 [8192, 4096], P(('seq', 'head'))
All inputs are finite; a program needn't handle non-finite values.
Results may differ from a plain program's by a relative error of at most 0.0036.
Values may be sent and summed in bfloat16 or wider, within the bound.
A program may use at most 128 MiB of HBM per device.

v0:
```python
import jax
import jax.numpy as jnp
from jax import lax
from jax.sharding import PartitionSpec as P

HQ = 32
KV = 16
HD = 128
WINDOW = 1024


score_scale = 168.0 ** (-0.5)
neg_fill = -1e30


def passed_along(value, axis, steps):
    count = lax.axis_size(axis)
    first, last = (max(0, -steps), min(count, count - steps))
    return lax.ppermute(value, axis, [(source, source + steps) for source in range(first, last)])


def on_device(queries, key_rows, value_rows):
    parts_head = lax.axis_size("head")
    block = queries.shape[0] * parts_head
    rows = min(512, block)
    group = HQ // KV
    head_q, head_k, head_v = (
        lax.all_to_all(queries, "head", split_axis=1, concat_axis=0, tiled=True),
        lax.all_to_all(key_rows, "head", split_axis=1, concat_axis=0, tiled=True),
        lax.all_to_all(value_rows, "head", split_axis=1, concat_axis=0, tiled=True),
    )
    tail_pair = jnp.stack([head_k[block - WINDOW :], head_v[block - WINDOW :]])
    earlier = passed_along(tail_pair, "seq", 1)
    prior_k = earlier[0]
    prior_v = earlier[1]
    local_kv = head_k.shape[1] // HD
    local_q = local_kv * group
    anchor = lax.axis_index("seq") * block
    block_count = block // rows

    def attend(source_k, source_v, key_base, index_block):
        start = index_block * rows
        query_tile = lax.dynamic_slice_in_dim(head_q, start, rows, 0).reshape(
            rows, local_kv, group, HD
        )
        key_start = start - key_base
        key_tile = lax.dynamic_slice_in_dim(source_k, key_start, rows + WINDOW, 0).reshape(
            rows + WINDOW, local_kv, HD
        )
        value_tile = lax.dynamic_slice_in_dim(source_v, key_start, rows + WINDOW, 0).reshape(
            rows + WINDOW, local_kv, HD
        )
        scores = (
            jnp.einsum("qgrd,kgd->grqk", query_tile, key_tile, preferred_element_type=jnp.float32)
            * score_scale
        )
        query_pos = anchor + start + jnp.arange(rows, dtype=jnp.int32)
        key_pos = anchor + start - WINDOW + jnp.arange(rows + WINDOW, dtype=jnp.int32)
        spacing = query_pos[:, None] - key_pos[None, :]
        allowed = (spacing >= 0) & (spacing < WINDOW) & (key_pos[None, :] >= 0)
        scores = jnp.where(allowed, scores, jnp.float32(neg_fill))
        peak = jnp.max(scores, axis=-1, keepdims=True)
        expo = jnp.exp(scores - peak)
        total = jnp.sum(expo, axis=-1)
        weights = expo.astype(jnp.bfloat16)
        mixed = jnp.einsum(
            "grqk,kgd->qgrd", weights, value_tile, preferred_element_type=jnp.float32
        )
        mixed = mixed / jnp.transpose(total, (2, 0, 1))[..., None]
        return mixed.reshape(rows, local_q * HD).astype(jnp.bfloat16)

    extended_k = jnp.concatenate([prior_k, head_k], axis=0)
    extended_v = jnp.concatenate([prior_v, head_v], axis=0)
    head_out = lax.map(
        lambda index_block: attend(extended_k, extended_v, 0, index_block),
        jnp.arange(block_count, dtype=jnp.int32),
    ).reshape(block, local_q * HD)
    return lax.all_to_all(head_out, "head", split_axis=0, concat_axis=1, tiled=True)


def solution(mesh):
    placed = (P(("seq", "head"), None), P(("seq", "head"), None), P(("seq", "head"), None))
    return jax.shard_map(
        on_device, mesh=mesh, in_specs=placed, out_specs=P(("seq", "head"), None), check_vma=False
    )
```

profile of v0, /device:TPU:24, one launch (start us, length us, event | category | flops | bytes accessed | tf_op | source)
XLA Modules:
  0.0 233.9 jit_solution(1045873459218599841)
XLA Ops:
  0.0 2.3 copy.37
  2.3 3.5 %all-to-all-start = ((bf16[256,4,512]{0,2,1:T(8,128)(2,1)}), bf16[256,4,512]{0,2,1:T(8,128)(2,1)S(1)}, u32[]{:S(2)}, u32[]{:S(2)}) async-start(bf16[256,4,512]{0,2,1:T(8,128)(2,1)} %bitcast.11), calls=%async_computation | async-start | bytes 2097152 | tf_op jit(solution)/shard_map/all_to_all | solution.py:29
  7.2 13.1 %all-to-all-done = bf16[256,4,512]{0,2,1:T(8,128)(2,1)S(1)} async-done(((bf16[256,4,512]{0,2,1:T(8,128)(2,1)}), bf16[256,4,512]{0,2,1:T(8,128)(2,1)S(1)}, u32[]{:S(2)}, u32[]{:S(2)}) %all-to-all-start) | async-done | bytes 1048608 | tf_op jit(solution)/shard_map/all_to_all | solution.py:29
  20.3 3.5 %all-to-all-start.1 = ((bf16[256,4,512]{0,2,1:T(8,128)(2,1)}), bf16[256,4,512]{0,2,1:T(8,128)(2,1)S(1)}, u32[]{:S(2)}, u32[]{:S(2)}) async-start(bf16[256,4,512]{0,2,1:T(8,128)(2,1)} %bitcast.14), calls=%async_computation.1 | async-start | bytes 2097152 | tf_op jit(solution)/shard_map/all_to_all | solution.py:30
  24.4 13.9 %all-to-all-done.1 = bf16[256,4,512]{0,2,1:T(8,128)(2,1)S(1)} async-done(((bf16[256,4,512]{0,2,1:T(8,128)(2,1)}), bf16[256,4,512]{0,2,1:T(8,128)(2,1)S(1)}, u32[]{:S(2)}, u32[]{:S(2)}) %all-to-all-start.1) | async-done | bytes 1048608 | tf_op jit(solution)/shard_map/all_to_all | solution.py:30
  38.8 1.5 pad_maximum_fusion
  40.3 3.4 %collective-permute-start = (bf16[2,1024,512]{2,1,0:T(8,128)(2,1)}, bf16[2,1024,512]{2,1,0:T(8,128)(2,1)}, u32[]{:S(2)}, u32[]{:S(2)}) collective-permute-start(bf16[2,1024,512]{2,1,0:T(8,128)(2,1)} %pad_maximum_fusion), channel_id=1, source_target_pairs={{0,4},{4,8},{8,12},{12,16},{16,20},{20,24},{24,28},{1,5},{5,9},{9,... | collective-permute-start | bytes 6291464 | tf_op jit(solution)/shard_map/ppermute | solution.py:19
  43.7 4.1 %copy.41 = bf16[256,4096]{0,1:T(8,128)(2,1)} copy(bf16[256,4096]{1,0:T(8,128)(2,1)} %param.5) | data formatting | bytes 4194304 | tf_op args[0]
  47.8 4.5 %all-to-all-start.2 = ((bf16[256,4,1024]{0,2,1:T(8,128)(2,1)}), bf16[256,4,1024]{0,2,1:T(8,128)(2,1)}, u32[]{:S(2)}, u32[]{:S(2)}) async-start(bf16[256,4,1024]{0,2,1:T(8,128)(2,1)} %bitcast.75), calls=%async_computation.2 | async-start | bytes 4194304 | tf_op jit(solution)/shard_map/all_to_all | solution.py:28
  52.3 25.7 %all-to-all-done.2 = bf16[256,4,1024]{0,2,1:T(8,128)(2,1)} async-done(((bf16[256,4,1024]{0,2,1:T(8,128)(2,1)}), bf16[256,4,1024]{0,2,1:T(8,128)(2,1)}, u32[]{:S(2)}, u32[]{:S(2)}) %all-to-all-start.2) | async-done | bytes 2097184 | tf_op jit(solution)/shard_map/all_to_all | solution.py:28
  78.1 4.0 %copy.42 = bf16[256,4,1024]{2,0,1:T(8,128)(2,1)} copy(bf16[256,4,1024]{0,2,1:T(8,128)(2,1)} %all-to-all-done.2) | data formatting | bytes 4194304 | tf_op jit(solution)/shard_map/all_to_all | solution.py:28
  82.1 8.5 %collective-permute-done = bf16[2,1024,512]{2,1,0:T(8,128)(2,1)} collective-permute-done((bf16[2,1024,512]{2,1,0:T(8,128)(2,1)}, bf16[2,1024,512]{2,1,0:T(8,128)(2,1)}, u32[]{:S(2)}, u32[]{:S(2)}) %collective-permute-start) | collective-permute-done | bytes 2097184 | tf_op jit(solution)/shard_map/ppermute | solution.py:19
  90.6 1.7 slice_bitcast_fusion
  92.3 2.3 pad_maximum_fusion.1
  94.6 103.4 %while.12 = (s32[]{:T(128)}, bf16[2,512,1024]{2,1,0:T(8,128)(2,1)}, s32[2]{0:T(128)S(1)}, bf16[2048,512]{1,0:T(8,128)(2,1)}, s32[]{:T(128)}, /*index=5*/bf16[204...) while((s32[]{:T(128)}, bf16[2,512,1024]{2,1,0:T(8,128)(2,1)}, ...), condition=%wide.region_3.4_spmd, body=%wide.region_0.3_spmd.sunk | while | flops 3270243328 | bytes 123309384 | solution.py:74
  95.8 2.0 fusion.26
  97.7 2.1 constant_dynamic-slice_fusion.5
  99.8 1.6 copy.65
  104.1 14.5 %fusion.27 = (f32[4,2,512]{2,1,0:T(2,128)S(1)}, f32[4,2,512,1536]{2,3,1,0:T(8,128)}) fusion(bf16[1536,4,128,1]{0,2,3,1:T(8,128)(2,1)} %bitcast.68, bf16[512,4,2,128]{0,3,2,1:T(8,128)(2,1)} %bitcast.69, pred[512,1536]{0,1:T(8,128)(4,1)S(1)} %copy-done), kind=kOutput, calls=%fused_computation.24.clone.1 | convolution fusion | flops 1629483008 | bytes 28590080 | tf_op jit(solution)/shard_map/while/body/eval_jaxpr/qgrd,kgd->grqk/dot_general | solution.py:54
  118.6 10.1 %fusion.28 = f32[4,2,512]{2,1,0:T(2,128)S(1)} fusion(f32[4,2,512,1536]{2,3,1,0:T(8,128)} %get-tuple-element.180, f32[4,2,512]{2,1,0:T(2,128)S(1)} %get-tuple-element.181), kind=kLoop, calls=%fused_computation.2.clone.1 | loop fusion | flops 12578816 | bytes 25198592 | tf_op jit(solution)/shard_map/while/body/eval_jaxpr/reduce_sum | solution.py:64
  129.5 13.5 %fusion.29 = bf16[512,4,2,128]{0,3,2,1:T(8,128)(2,1)} fusion(bf16[1536,4,128,1]{0,2,3,1:T(8,128)(2,1)S(1)} %bitcast.66, f32[4,2,512,1536]{2,3,1,0:T(8,128)} %get-tuple-element.180, f32[4,2,512]{2,1,0:T(2,128)S(1)} %get-tuple-element.181, f32[512,4,2]{0,2,1:T(2,128)S(1)} %bitcast.79), kind=kOutput, calls=%fused_computation.11.clone.1 | convolution fusion | flops 1624244224 | bytes 27820032 | tf_op jit(solution)/shard_map/while/body/eval_jaxpr/grqk,kgd->qgrd/dot_general | solution.py:66
  143.0 1.6 copy.67
  147.5 2.0 fusion.26
  149.5 2.1 constant_dynamic-slice_fusion.5
  151.5 1.6 copy.65
  155.9 14.5 %fusion.27 = (f32[4,2,512]{2,1,0:T(2,128)S(1)}, f32[4,2,512,1536]{2,3,1,0:T(8,128)}) fusion(bf16[1536,4,128,1]{0,2,3,1:T(8,128)(2,1)} %bitcast.68, bf16[512,4,2,128]{0,3,2,1:T(8,128)(2,1)} %bitcast.69, pred[512,1536]{0,1:T(8,128)(4,1)S(1)} %copy-done), kind=kOutput, calls=%fused_computation.24.clone.1 | convolution fusion | flops 1629483008 | bytes 28590080 | tf_op jit(solution)/shard_map/while/body/eval_jaxpr/qgrd,kgd->grqk/dot_general | solution.py:54
  170.4 10.1 %fusion.28 = f32[4,2,512]{2,1,0:T(2,128)S(1)} fusion(f32[4,2,512,1536]{2,3,1,0:T(8,128)} %get-tuple-element.180, f32[4,2,512]{2,1,0:T(2,128)S(1)} %get-tuple-element.181), kind=kLoop, calls=%fused_computation.2.clone.1 | loop fusion | flops 12578816 | bytes 25198592 | tf_op jit(solution)/shard_map/while/body/eval_jaxpr/reduce_sum | solution.py:64
  181.2 13.5 %fusion.29 = bf16[512,4,2,128]{0,3,2,1:T(8,128)(2,1)} fusion(bf16[1536,4,128,1]{0,2,3,1:T(8,128)(2,1)S(1)} %bitcast.66, f32[4,2,512,1536]{2,3,1,0:T(8,128)} %get-tuple-element.180, f32[4,2,512]{2,1,0:T(2,128)S(1)} %get-tuple-element.181, f32[512,4,2]{0,2,1:T(2,128)S(1)} %bitcast.79), kind=kOutput, calls=%fused_computation.11.clone.1 | convolution fusion | flops 1624244224 | bytes 27820032 | tf_op jit(solution)/shard_map/while/body/eval_jaxpr/grqk,kgd->qgrd/dot_general | solution.py:66
  194.7 1.6 copy.67
  198.0 29.3 %all_to_all.76 = bf16[4,256,1024]{2,1,0:T(8,128)(2,1)S(1)} all-to-all(bf16[4,256,1024]{2,1,0:T(8,128)(2,1)} %bitcast.78), channel_id=1, replica_groups=mesh['seq'=8,'head'=4] {'head'}, dimensions={0} | all-to-all | bytes 4194304 | tf_op jit(solution)/shard_map/all_to_all | solution.py:78
  227.3 2.6 %copy.47 = bf16[256,4,1024]{0,2,1:T(8,128)(2,1)} copy(bf16[256,4,1024]{2,0,1:T(8,128)(2,1)S(1)} %bitcast.76) | data formatting | bytes 4194304 | tf_op jit(solution)/shard_map/all_to_all | solution.py:78
  229.9 4.1 %copy.48 = bf16[256,4096]{1,0:T(8,128)(2,1)} copy(bf16[256,4096]{0,1:T(8,128)(2,1)} %bitcast.77) | data formatting | bytes 4194304 | tf_op jit(solution)/shard_map/all_to_all | solution.py:78
  (35 shorter events, 13.8 us)
Async XLA Ops:
  0.0 5.9 %copy-start.3 = (bf16[256,2048]{1,0:T(8,128)(2,1)S(1)}, bf16[256,2048]{1,0:T(8,128)(2,1)}, u32[]{:S(2)}) copy-start(bf16[256,2048]{1,0:T(8,128)(2,1)} %param.7) | copy-start | bytes 3145732
  2.3 18.0 %all-to-all-start = ((bf16[256,4,512]{0,2,1:T(8,128)(2,1)}), bf16[256,4,512]{0,2,1:T(8,128)(2,1)S(1)}, u32[]{:S(2)}, u32[]{:S(2)}) async-start(bf16[256,4,512]{0,2,1:T(8,128)(2,1)} %bitcast.11), calls=%async_computation | async-start | bytes 2097152 | tf_op jit(solution)/shard_map/all_to_all | solution.py:29
  20.3 18.0 %all-to-all-start.1 = ((bf16[256,4,512]{0,2,1:T(8,128)(2,1)}), bf16[256,4,512]{0,2,1:T(8,128)(2,1)S(1)}, u32[]{:S(2)}, u32[]{:S(2)}) async-start(bf16[256,4,512]{0,2,1:T(8,128)(2,1)} %bitcast.14), calls=%async_computation.1 | async-start | bytes 2097152 | tf_op jit(solution)/shard_map/all_to_all | solution.py:30
  40.3 50.3 %collective-permute-start = (bf16[2,1024,512]{2,1,0:T(8,128)(2,1)}, bf16[2,1024,512]{2,1,0:T(8,128)(2,1)}, u32[]{:S(2)}, u32[]{:S(2)}) collective-permute-start(bf16[2,1024,512]{2,1,0:T(8,128)(2,1)} %pad_maximum_fusion), channel_id=1, source_target_pairs={{0,4},{4,8},{8,12},{12,16},{16,20},{20,24},{24,28},{1,5},{5,9},{9,... | collective-permute-start | bytes 6291464 | tf_op jit(solution)/shard_map/ppermute | solution.py:19
  47.8 30.2 %all-to-all-start.2 = ((bf16[256,4,1024]{0,2,1:T(8,128)(2,1)}), bf16[256,4,1024]{0,2,1:T(8,128)(2,1)}, u32[]{:S(2)}, u32[]{:S(2)}) async-start(bf16[256,4,1024]{0,2,1:T(8,128)(2,1)} %bitcast.75), calls=%async_computation.2 | async-start | bytes 4194304 | tf_op jit(solution)/shard_map/all_to_all | solution.py:28
  101.4 2.7 %copy-start = (pred[512,1536]{0,1:T(8,128)(4,1)S(1)}, pred[512,1536]{0,1:T(8,128)(4,1)}, u32[]{:S(2)}) copy-start(pred[512,1536]{0,1:T(8,128)(4,1)} %fusion.26) | copy-start | bytes 2359300 | tf_op jit(solution)/shard_map/while
  143.0 1.9 copy-start.1
  145.0 1.3 copy-start.2
  153.1 2.7 %copy-start = (pred[512,1536]{0,1:T(8,128)(4,1)S(1)}, pred[512,1536]{0,1:T(8,128)(4,1)}, u32[]{:S(2)}) copy-start(pred[512,1536]{0,1:T(8,128)(4,1)} %fusion.26) | copy-start | bytes 2359300 | tf_op jit(solution)/shard_map/while
  194.7 1.9 copy-start.1
  196.7 1.3 copy-start.2
where the time goes:
time: 235 us; the launch traced here: 234 us
  waiting for transfers between devices  61.2 us (26%)
  matrix products  56 us (24%)
  local copies, waits for them, and re-layouts  43.2 us (18%)
  blocking collectives  29.3 us (12%)
  other arithmetic  28 us (12%)
  starting transfers between devices  14.9 us (6%)
    all_to_all x1, blocking collectives, on_device(): lax.all_to_all(head_out, 'head', split_axis=0, concat_axis=1, tiled=True)  29.3 us
    dot_general x2, matrix products, attend(): jnp.einsum('qgrd,kgd->grqk', query_tile, key_tile, preferred_element_type...  29 us
    dot_general x2, matrix products, attend(): jnp.einsum('grqk,kgd->qgrd', weights, value_tile, preferred_element_type=...  27 us
    all_to_all x1, waiting for transfers between devices, on_device(): lax.all_to_all(queries, 'head', split_axis=1, concat_axis=0, tiled=True)  25.7 us
    reduce_sum x2, other arithmetic, attend(): total = jnp.sum(expo, axis=-1)  20.2 us
    all_to_all x1, waiting for transfers between devices, on_device(): lax.all_to_all(value_rows, 'head', split_axis=1, concat_axis=0, tiled=True)  13.9 us
    all_to_all x1, waiting for transfers between devices, on_device(): lax.all_to_all(key_rows, 'head', split_axis=1, concat_axis=0, tiled=True)  13.1 us
    ppermute x1, waiting for transfers between devices, passed_along(): lax.ppermute(value, axis, [(source, source + steps) for source in range(f...  8.51 us
  transfers between devices with their start and end apart: 4, of which 4 were waited for; matrix products, arithmetic and copies ran while one was open for 4% of the time, Pallas kernels for 0%

commit v1 on v0

v1 whole, which is shorter than its diff:
```python
import functools
import math

import jax
import jax.numpy as jnp
from jax import lax
from jax.experimental import pallas as pl
from jax.experimental.pallas import tpu as pltpu
from jax.sharding import PartitionSpec as P

HQ = 32
KV = 16
HD = 128
WINDOW = 1024
GROUP = HQ // KV
CHUNKS = 8

MESH = pl.DeviceIdType.MESH
exponent_scale = 168.0 ** (-0.5) * math.log2(math.e)
neg_fill = -1e30


def kernel(
    count,
    n_head,
    q_hbm,
    k_hbm,
    v_hbm,
    out_hbm,
    q_buf,
    k_buf,
    v_buf,
    out_buf,
    q_sem,
    own_sem,
    out_sem,
    send_sem,
    recv_sem,
):
    rows = q_hbm.shape[0]
    back = WINDOW // rows
    heads = KV // CHUNKS
    width = heads * HD
    me = lax.axis_index("seq") * n_head + lax.axis_index("head")
    core = lax.rem(me, 2)
    odd_chip = lax.rem(me // 2, 2)
    sibling = me + 1 - 2 * core
    across = me + 2 - 4 * odd_chip
    has_next = me + back < count
    has_far = me >= back
    has_mid = me >= 2

    def place(rank):
        return (rank // n_head, lax.rem(rank, n_head))

    def columns(g):
        return pl.ds(pl.multiple_of(g * width, width), width)

    def slot(distance):
        return pl.ds((back - distance) * rows, rows)

    own = (k_hbm, v_hbm)
    held = (k_buf, v_buf)

    def send(kind, g, which, source, distance, target):
        if source == 0:
            src = own[which].at[:, columns(g)]
        else:
            src = held[which].at[slot(source), columns(g)]
        return pltpu.make_async_remote_copy(
            src_ref=src,
            dst_ref=held[which].at[slot(distance), columns(g)],
            send_sem=send_sem.at[kind, g, which],
            recv_sem=recv_sem.at[distance - 1, g, which],
            device_id=place(target),
            device_id_type=MESH,
        )

    def sends(g):
        return {
            "next": (has_next, 0, 0, back, me + back),
            "core": (core == 0, 1, 0, 1, sibling),
            "up": (odd_chip == 0, 2, 0, 2, across),
            "down": ((odd_chip == 1) & has_far, 2, back, 2, across),
            "far": ((core == 1) & has_far, 3, back, 3, sibling),
            "mid0": ((core == 0) & has_mid, 4, 2, 3, sibling),
            "mid1": ((core == 1) & has_mid, 4, 2, 1, sibling),
        }

    def start(g, *names):
        for name in names:
            condition, kind, source, distance, target = sends(g)[name]

            @pl.when(condition)
            def _():
                for which in range(2):
                    send(kind, g, which, source, distance, target).start()

    def arrived(g, distance):
        for which in range(2):
            send(0, g, which, distance, distance, sibling).wait_recv()

    def load_own(g, which):
        return pltpu.make_async_copy(
            own[which].at[:, columns(g)], held[which].at[slot(0), columns(g)], own_sem.at[g, which]
        )

    def q_columns(g):
        return pl.ds(pl.multiple_of(g * width * GROUP, width * GROUP), width * GROUP)

    def load_q(g):
        return pltpu.make_async_copy(q_hbm.at[:, q_columns(g)], q_buf.at[:, q_columns(g)], q_sem.at[g])

    def store_out(g):
        return pltpu.make_async_copy(
            out_buf.at[:, q_columns(g)], out_hbm.at[:, q_columns(g)], out_sem.at[g]
        )

    def attend(g, checked):
        row = lax.broadcasted_iota(jnp.int32, (rows, rows), 0)
        column = lax.broadcasted_iota(jnp.int32, (rows, rows), 1)
        for local in range(heads):
            head = g * heads + local
            at = pl.ds(pl.multiple_of(head * HD, HD), HD)
            keys = k_buf[:, at]
            values = v_buf[:, at]
            for r in range(GROUP):
                q_at = pl.ds(pl.multiple_of((head * GROUP + r) * HD, HD), HD)
                scores = lax.dot_general(
                    q_buf[:, q_at], keys, (((1,), (1,)), ((), ())), preferred_element_type=jnp.float32
                )
                pieces = []
                for j in range(back + 1):
                    piece = scores[:, j * rows : (j + 1) * rows]
                    keep = None
                    if j == 0:
                        keep = column > row
                    elif j == back:
                        keep = column <= row
                    if checked and j < back:
                        there = jnp.full((rows, rows), me - back + j, jnp.int32) >= 0
                        keep = there if keep is None else keep & there
                    pieces.append(piece if keep is None else jnp.where(keep, piece, neg_fill))
                scores = jnp.concatenate(pieces, axis=1)
                peak = jnp.max(scores, axis=1, keepdims=True)
                expo = jnp.exp2((scores - peak) * exponent_scale)
                total = jnp.sum(expo, axis=1, keepdims=True)
                mixed = jnp.dot(expo.astype(jnp.bfloat16), values, preferred_element_type=jnp.float32)
                out_buf[:, q_at] = (mixed / total).astype(jnp.bfloat16)

    barrier = pltpu.get_barrier_semaphore()
    for target in (sibling, across):
        pl.semaphore_signal(barrier, inc=1, device_id=place(target), device_id_type=MESH)

    @pl.when(has_next)
    def _():
        pl.semaphore_signal(barrier, inc=1, device_id=place(me + back), device_id_type=MESH)

    @pl.when(has_far)
    def _():
        pl.semaphore_signal(barrier, inc=1, device_id=place(me - back), device_id_type=MESH)

    for distance in range(1, back + 1):

        @pl.when(me < distance)
        def _():
            for which in range(2):
                held[which][slot(distance), :] = jnp.zeros((rows, KV * HD), jnp.bfloat16)

    pl.semaphore_wait(barrier, 2 + has_next.astype(jnp.int32) + has_far.astype(jnp.int32))

    @pl.loop(0, CHUNKS)
    def _(g):
        start(g, "next", "up", "core")

    @pl.loop(0, CHUNKS)
    def _(g):
        load_q(g).start()
        for which in range(2):
            load_own(g, which).start()

    @pl.loop(0, CHUNKS + 2)
    def _(t):
        @pl.when((t < CHUNKS) & has_far)
        def _():
            arrived(t, back)
            start(t, "down", "far")

        mid = t - 1

        @pl.when((mid >= 0) & (mid < CHUNKS) & has_mid)
        def _():
            arrived(mid, 2)
            start(mid, "mid0", "mid1")

        g = t - 2

        @pl.when(g >= 0)
        def _():
            @pl.when(me >= 1)
            def _():
                arrived(g, 1)

            @pl.when(me >= 3)
            def _():
                arrived(g, 3)

            load_q(g).wait()
            for which in range(2):
                load_own(g, which).wait()

            @pl.when(has_far)
            def _():
                attend(g, False)

            @pl.when(me < back)
            def _():
                attend(g, True)

            store_out(g).start()

    @pl.loop(0, CHUNKS)
    def _(g):
        store_out(g).wait()
        for condition, kind, source, distance, target in sends(g).values():

            @pl.when(condition)
            def _():
                for which in range(2):
                    send(kind, g, which, source, distance, target).wait_send()


def solution(mesh):
    n_head = mesh.shape["head"]
    count = mesh.shape["seq"] * n_head

    def on_device(queries, key_rows, value_rows):
        rows = queries.shape[0]
        assert rows * 4 == WINDOW and n_head % 4 == 0
        span = rows + WINDOW
        return pl.pallas_call(
            functools.partial(kernel, count, n_head),
            out_shape=jax.ShapeDtypeStruct(queries.shape, queries.dtype),
            in_specs=[pl.BlockSpec(memory_space=pl.ANY)] * 3,
            out_specs=pl.BlockSpec(memory_space=pl.ANY),
            scratch_shapes=[
                pltpu.VMEM(queries.shape, jnp.bfloat16),
                pltpu.VMEM((span, KV * HD), jnp.bfloat16),
                pltpu.VMEM((span, KV * HD), jnp.bfloat16),
                pltpu.VMEM(queries.shape, jnp.bfloat16),
                pltpu.SemaphoreType.DMA((CHUNKS,)),
                pltpu.SemaphoreType.DMA((CHUNKS, 2)),
                pltpu.SemaphoreType.DMA((CHUNKS,)),
                pltpu.SemaphoreType.DMA((5, CHUNKS, 2)),
                pltpu.SemaphoreType.DMA((4, CHUNKS, 2)),
            ],
            compiler_params=pltpu.CompilerParams(
                collective_id=0, has_side_effects=True, vmem_limit_bytes=60 * 1024 * 1024
            ),
            cost_estimate=pl.CostEstimate(
                flops=4 * HQ * rows * span * HD,
                bytes_accessed=16 * 1024 * 1024,
                transcendentals=HQ * rows * span,
            ),
        )(queries, key_rows, value_rows)

    placed = P(("seq", "head"), None)
    return jax.shard_map(
        on_device, mesh=mesh, in_specs=(placed, placed, placed), out_specs=placed, check_vma=False
    )
```

time: 235 us -> 66.2 us (0.28)
  Pallas kernels: 0 us -> 62.9 us
  waiting for transfers between devices: 61.2 us -> 0 us
  matrix products: 56 us -> 0 us
  local copies, waits for them, and re-layouts: 43.2 us -> 3.13 us
  blocking collectives: 29.3 us -> 0 us
  other arithmetic: 28 us -> 0 us
  starting transfers between devices: 14.9 us -> 0 us
    pallas_call x0 -> x1, Pallas kernels: none -> 62.9 us  [on_device(): pl.pallas_call(functools.partial(kernel, count, n_head), out_shape=jax.Sh...]
    dot_general x4 -> x0, matrix products: 56 us -> none  [the longest x2 29 us: attend(): jnp.einsum('qgrd,kgd->grqk', query_tile, key_tile, preferred_element_type...]
    all_to_all x3 -> x0, waiting for transfers between devices: 52.7 us -> none  [the longest x1 25.7 us: on_device(): lax.all_to_all(queries, 'head', split_axis=1, concat_axis=0, tiled=True)]
    all_to_all x1 -> x0, blocking collectives: 29.3 us -> none  [on_device(): lax.all_to_all(head_out, 'head', split_axis=0, concat_axis=1, tiled=True)]
    reduce_sum x2 -> x0, other arithmetic: 20.2 us -> none  [attend(): total = jnp.sum(expo, axis=-1)]
    dynamic_slice x12 -> x0, local copies, waits for them, and re-layouts: 15.4 us -> none  [the longest x4 7.35 us: attend(): lax.dynamic_slice_in_dim(source_k, key_start, rows + WINDOW, 0)]
    all_to_all x5 -> x0, local copies, waits for them, and re-layouts: 11.7 us -> none  [the longest x2 6.62 us: on_device(): lax.all_to_all(head_out, 'head', split_axis=0, concat_axis=1, tiled=True)]
    all_to_all x3 -> x0, starting transfers between devices: 11.5 us -> none  [the longest x1 4.45 us: on_device(): lax.all_to_all(queries, 'head', split_axis=1, concat_axis=0, tiled=True)]
  transfers between devices with their start and end apart: 4 -> 0, of which waited for: 4 -> 0; matrix products, arithmetic and copies ran while one was open for 4% -> 0% of each run, Pallas kernels for 0% -> 0%
where the time goes in v1:
time: 66.2 us; the launch traced here: 66.1 us
  Pallas kernels  62.9 us (95%)
  local copies, waits for them, and re-layouts  3.13 us (5%)
    pallas_call x1, Pallas kernels, on_device(): pl.pallas_call(functools.partial(kernel, count, n_head), out_shape=jax.Sh...  62.9 us
    unnamed x1, local copies, waits for them, and re-layouts  3.13 us

profile of v1, /device:TPU:24, one launch (start us, length us, event | category | flops | bytes accessed | tf_op | source)
XLA Modules:
  0.0 66.1 jit_solution(7639811898440722766)
XLA Ops:
  0.0 62.9 %shard_map.37 = bf16[256,4096]{1,0:T(8,128)(2,1)} custom-call(bf16[256,4096]{1,0:T(8,128)(2,1)} %q_hbm.1, bf16[256,2048]{1,0:T(8,128)(2,1)} %k_hbm.1, bf16[256,2048]{1,0:T(8,128)(2,1)} %v_hbm.1), custom_call_target="tpu_custom_call" | custom-call | flops 5368709120 | bytes 16777216 | tf_op jit(solution)/shard_map/pallas_call | solution.py:241
  62.9 3.1 %copy.5 = bf16[256,4096]{1,0:T(8,128)(2,1)} copy(bf16[256,4096]{1,0:T(8,128)(2,1)} %shard_map.37) | data formatting | bytes 4194304

commit v2 on v1

--- a/solution.py
+++ b/solution.py
@@ -13,7 +13,8 @@
 HD = 128
 WINDOW = 1024
 GROUP = HQ // KV
-CHUNKS = 8
+CHUNKS = 16
+AHEAD = 4
 
 MESH = pl.DeviceIdType.MESH
 exponent_scale = 168.0 ** (-0.5) * math.log2(math.e)
@@ -34,6 +35,7 @@
     q_sem,
     own_sem,
     out_sem,
+    core_sem,
     send_sem,
     recv_sem,
 ):
@@ -70,7 +72,7 @@
         return pltpu.make_async_remote_copy(
             src_ref=src,
             dst_ref=held[which].at[slot(distance), columns(g)],
-            send_sem=send_sem.at[kind, g, which],
+            send_sem=send_sem.at[kind, which],
             recv_sem=recv_sem.at[distance - 1, g, which],
             device_id=place(target),
             device_id_type=MESH,
@@ -79,41 +81,46 @@
     def sends(g):
         return {
             "next": (has_next, 0, 0, back, me + back),
-            "core": (core == 0, 1, 0, 1, sibling),
-            "up": (odd_chip == 0, 2, 0, 2, across),
-            "down": ((odd_chip == 1) & has_far, 2, back, 2, across),
-            "far": ((core == 1) & has_far, 3, back, 3, sibling),
-            "mid0": ((core == 0) & has_mid, 4, 2, 3, sibling),
-            "mid1": ((core == 1) & has_mid, 4, 2, 1, sibling),
+            "up": (odd_chip == 0, 1, 0, 2, across),
+            "down": ((odd_chip == 1) & has_far, 1, back, 2, across),
+            "far": ((core == 1) & has_far, 2, back, 3, sibling),
+            "mid0": ((core == 0) & has_mid, 3, 2, 3, sibling),
+            "mid1": ((core == 1) & has_mid, 3, 2, 1, sibling),
         }
 
-    def start(g, *names):
+    def start(g, which, *names):
         for name in names:
             condition, kind, source, distance, target = sends(g)[name]
 
             @pl.when(condition)
             def _():
-                for which in range(2):
-                    send(kind, g, which, source, distance, target).start()
-
-    def arrived(g, distance):
-        for which in range(2):
-            send(0, g, which, distance, distance, sibling).wait_recv()
-
-    def load_own(g, which):
-        return pltpu.make_async_copy(
-            own[which].at[:, columns(g)], held[which].at[slot(0), columns(g)], own_sem.at[g, which]
+                send(kind, g, which, source, distance, target).start()
+
+    def arrived(g, which, distance):
+        send(0, g, which, distance, distance, sibling).wait_recv()
+
+    def load_own(which):
+        return pltpu.make_async_copy(own[which], held[which].at[slot(0), :], own_sem.at[which])
+
+    def send_core(which):
+        return pltpu.make_async_remote_copy(
+            src_ref=own[which],
+            dst_ref=held[which].at[slot(1), :],
+            send_sem=core_sem.at[0, which],
+            recv_sem=core_sem.at[1, which],
+            device_id=place(sibling),
+            device_id_type=MESH,
         )
 
     def q_columns(g):
         return pl.ds(pl.multiple_of(g * width * GROUP, width * GROUP), width * GROUP)
 
-    def load_q(g):
-        return pltpu.make_async_copy(q_hbm.at[:, q_columns(g)], q_buf.at[:, q_columns(g)], q_sem.at[g])
+    def load_q():
+        return pltpu.make_async_copy(q_hbm, q_buf, q_sem)
 
     def store_out(g):
         return pltpu.make_async_copy(
-            out_buf.at[:, q_columns(g)], out_hbm.at[:, q_columns(g)], out_sem.at[g]
+            out_buf.at[:, q_columns(g)], out_hbm.at[:, q_columns(g)], out_sem
         )
 
     def attend(g, checked):
@@ -160,6 +167,24 @@
     def _():
         pl.semaphore_signal(barrier, inc=1, device_id=place(me - back), device_id_type=MESH)
 
+    pl.semaphore_wait(barrier, 2 + has_next.astype(jnp.int32) + has_far.astype(jnp.int32))
+
+    def start_own(g):
+        for which in range(2):
+            start(g, which, "next", "up")
+
+    for g in range(AHEAD):
+        start_own(g)
+
+    @pl.when(core == 0)
+    def _():
+        for which in range(2):
+            send_core(which).start()
+
+    load_q().start()
+    for which in range(2):
+        load_own(which).start()
+
     for distance in range(1, back + 1):
 
         @pl.when(me < distance)
@@ -167,67 +192,82 @@
             for which in range(2):
                 held[which][slot(distance), :] = jnp.zeros((rows, KV * HD), jnp.bfloat16)
 
-    pl.semaphore_wait(barrier, 2 + has_next.astype(jnp.int32) + has_far.astype(jnp.int32))
-
-    @pl.loop(0, CHUNKS)
-    def _(g):
-        start(g, "next", "up", "core")
-
-    @pl.loop(0, CHUNKS)
-    def _(g):
-        load_q(g).start()
-        for which in range(2):
-            load_own(g, which).start()
-
     @pl.loop(0, CHUNKS + 2)
     def _(t):
+        @pl.when(t + AHEAD < CHUNKS)
+        def _():
+            start_own(t + AHEAD)
+
         @pl.when((t < CHUNKS) & has_far)
         def _():
-            arrived(t, back)
-            start(t, "down", "far")
+            for which in range(2):
+                arrived(t, which, back)
+                start(t, which, "down", "far")
 
         mid = t - 1
 
         @pl.when((mid >= 0) & (mid < CHUNKS) & has_mid)
         def _():
-            arrived(mid, 2)
-            start(mid, "mid0", "mid1")
+            for which in range(2):
+                arrived(mid, which, 2)
+                start(mid, which, "mid0", "mid1")
 
         g = t - 2
 
         @pl.when(g >= 0)
         def _():
-            @pl.when(me >= 1)
-            def _():
-                arrived(g, 1)
+            @pl.when((core == 0) & (me >= 1))
+            def _():
+                for which in range(2):
+                    arrived(g, which, 1)
+
+            @pl.when((core == 1) & (g == 0))
+            def _():
+                for which in range(2):
+                    send_core(which).wait_recv()
 
             @pl.when(me >= 3)
             def _():
-                arrived(g, 3)
-
-            load_q(g).wait()
+                for which in range(2):
+                    arrived(g, which, 3)
+
+            @pl.when(g == 0)
+            def _():
+                load_q().wait()
+                for which in range(2):
+                    load_own(which).wait()
+
+            @pl.when(has_far)
+            def _():
+                attend(g, False)
+
+            @pl.when(me < back)
+            def _():
+                attend(g, True)
+
+            store_out(g).start()
+
+    @pl.when(core == 0)
+    def _():
+        for which in range(2):
+            send_core(which).wait_send()
+
+    pltpu.make_async_copy(out_buf, out_hbm, out_sem).wait()
+    for kind, condition in enumerate(
+        (has_next, (odd_chip == 0) | has_far, (core == 1) & has_far, has_mid)
+    ):
+
+        @pl.when(condition)
+        def _():
             for which in range(2):
-                load_own(g, which).wait()
-
-            @pl.when(has_far)
-            def _():
-                attend(g, False)
-
-            @pl.when(me < back)
-            def _():
-                attend(g, True)
-
-            store_out(g).start()
-
-    @pl.loop(0, CHUNKS)
-    def _(g):
-        store_out(g).wait()
-        for condition, kind, source, distance, target in sends(g).values():
-
-            @pl.when(condition)
-            def _():
-                for which in range(2):
-                    send(kind, g, which, source, distance, target).wait_send()
+                pltpu.make_async_remote_copy(
+                    src_ref=own[which],
+                    dst_ref=held[which].at[slot(1), :],
+                    send_sem=send_sem.at[kind, which],
+                    recv_sem=core_sem.at[1, which],
+                    device_id=place(sibling),
+                    device_id_type=MESH,
+                ).wait_send()
 
 
 def solution(mesh):
@@ -248,10 +288,11 @@
                 pltpu.VMEM((span, KV * HD), jnp.bfloat16),
                 pltpu.VMEM((span, KV * HD), jnp.bfloat16),
                 pltpu.VMEM(queries.shape, jnp.bfloat16),
-                pltpu.SemaphoreType.DMA((CHUNKS,)),
-                pltpu.SemaphoreType.DMA((CHUNKS, 2)),
-                pltpu.SemaphoreType.DMA((CHUNKS,)),
-                pltpu.SemaphoreType.DMA((5, CHUNKS, 2)),
+                pltpu.SemaphoreType.DMA,
+                pltpu.SemaphoreType.DMA((2,)),
+                pltpu.SemaphoreType.DMA,
+                pltpu.SemaphoreType.DMA((2, 2)),
+                pltpu.SemaphoreType.DMA((4, 2)),
                 pltpu.SemaphoreType.DMA((4, CHUNKS, 2)),
             ],
             compiler_params=pltpu.CompilerParams(

time: 66.2 us -> 60.8 us (0.918)
  Pallas kernels: 62.9 us -> 57.5 us
    pallas_call x1, Pallas kernels: 62.9 us -> 57.5 us  [on_device(): pl.pallas_call(functools.partial(kernel, count, n_head), out_shape=jax.Sh...]
where the time goes in v2:
time: 60.8 us; the launch traced here: 60.7 us
  Pallas kernels  57.5 us (95%)
  local copies, waits for them, and re-layouts  3.13 us (5%)
    pallas_call x1, Pallas kernels, on_device(): pl.pallas_call(functools.partial(kernel, count, n_head), out_shape=jax.Sh...  57.5 us
    unnamed x1, local copies, waits for them, and re-layouts  3.13 us

profile of v2, /device:TPU:24, one launch (start us, length us, event | category | flops | bytes accessed | tf_op | source)
XLA Modules:
  0.0 60.7 jit_solution(4755792480234911619)
XLA Ops:
  0.0 57.5 %shard_map.37 = bf16[256,4096]{1,0:T(8,128)(2,1)} custom-call(bf16[256,4096]{1,0:T(8,128)(2,1)} %q_hbm.1, bf16[256,2048]{1,0:T(8,128)(2,1)} %k_hbm.1, bf16[256,2048]{1,0:T(8,128)(2,1)} %v_hbm.1), custom_call_target="tpu_custom_call" | custom-call | flops 5368709120 | bytes 16777216 | tf_op jit(solution)/shard_map/pallas_call | solution.py:281
  57.5 3.1 %copy.5 = bf16[256,4096]{1,0:T(8,128)(2,1)} copy(bf16[256,4096]{1,0:T(8,128)(2,1)} %shard_map.37) | data formatting | bytes 4194304

commit v3 on v2

--- a/solution.py
+++ b/solution.py
@@ -27,14 +27,12 @@
     q_hbm,
     k_hbm,
     v_hbm,
-    out_hbm,
+    out_ref,
     q_buf,
     k_buf,
     v_buf,
-    out_buf,
     q_sem,
     own_sem,
-    out_sem,
     core_sem,
     send_sem,
     recv_sem,
@@ -117,11 +115,6 @@
 
     def load_q():
         return pltpu.make_async_copy(q_hbm, q_buf, q_sem)
-
-    def store_out(g):
-        return pltpu.make_async_copy(
-            out_buf.at[:, q_columns(g)], out_hbm.at[:, q_columns(g)], out_sem
-        )
 
     def attend(g, checked):
         row = lax.broadcasted_iota(jnp.int32, (rows, rows), 0)
@@ -153,7 +146,7 @@
                 expo = jnp.exp2((scores - peak) * exponent_scale)
                 total = jnp.sum(expo, axis=1, keepdims=True)
                 mixed = jnp.dot(expo.astype(jnp.bfloat16), values, preferred_element_type=jnp.float32)
-                out_buf[:, q_at] = (mixed / total).astype(jnp.bfloat16)
+                out_ref[:, q_at] = (mixed / total).astype(jnp.bfloat16)
 
     barrier = pltpu.get_barrier_semaphore()
     for target in (sibling, across):
@@ -245,14 +238,11 @@
             def _():
                 attend(g, True)
 
-            store_out(g).start()
-
     @pl.when(core == 0)
     def _():
         for which in range(2):
             send_core(which).wait_send()
 
-    pltpu.make_async_copy(out_buf, out_hbm, out_sem).wait()
     for kind, condition in enumerate(
         (has_next, (odd_chip == 0) | has_far, (core == 1) & has_far, has_mid)
     ):
@@ -280,30 +270,28 @@
         span = rows + WINDOW
         return pl.pallas_call(
             functools.partial(kernel, count, n_head),
-            out_shape=jax.ShapeDtypeStruct(queries.shape, queries.dtype),
+            out_shape=pltpu.VMEM(queries.shape, queries.dtype),
             in_specs=[pl.BlockSpec(memory_space=pl.ANY)] * 3,
-            out_specs=pl.BlockSpec(memory_space=pl.ANY),
+            out_specs=pl.BlockSpec(memory_space=pltpu.VMEM),
             scratch_shapes=[
                 pltpu.VMEM(queries.shape, jnp.bfloat16),
                 pltpu.VMEM((span, KV * HD), jnp.bfloat16),
                 pltpu.VMEM((span, KV * HD), jnp.bfloat16),
-                pltpu.VMEM(queries.shape, jnp.bfloat16),
                 pltpu.SemaphoreType.DMA,
                 pltpu.SemaphoreType.DMA((2,)),
-                pltpu.SemaphoreType.DMA,
                 pltpu.SemaphoreType.DMA((2, 2)),
                 pltpu.SemaphoreType.DMA((4, 2)),
                 pltpu.SemaphoreType.DMA((4, CHUNKS, 2)),
             ],
             compiler_params=pltpu.CompilerParams(
-                collective_id=0, has_side_effects=True, vmem_limit_bytes=60 * 1024 * 1024
+                collective_id=0, has_side_effects=True, vmem_limit_bytes=48 * 1024 * 1024
             ),
             cost_estimate=pl.CostEstimate(
                 flops=4 * HQ * rows * span * HD,
                 bytes_accessed=16 * 1024 * 1024,
                 transcendentals=HQ * rows * span,
             ),
-        )(queries, key_rows, value_rows)
+        )(*(pltpu.with_memory_space_constraint(x, pltpu.HBM) for x in (queries, key_rows, value_rows)))
 
     placed = P(("seq", "head"), None)
     return jax.shard_map(

time: 60.8 us -> 58.3 us (0.959)
  local copies, waits for them, and re-layouts: 3.13 us -> 1.32 us
    unnamed x1, local copies, waits for them, and re-layouts: 3.13 us -> 1.32 us
    pallas_call x1, Pallas kernels: 57.5 us -> 56.9 us  [on_device(): pl.pallas_call(functools.partial(kernel, count, n_head), out_shape=pltpu....]
where the time goes in v3:
time: 58.3 us; the launch traced here: 58.2 us
  Pallas kernels  56.9 us (98%)
  local copies, waits for them, and re-layouts  1.32 us (2%)
    pallas_call x1, Pallas kernels, on_device(): pl.pallas_call(functools.partial(kernel, count, n_head), out_shape=pltpu....  56.9 us
    unnamed x1, local copies, waits for them, and re-layouts  1.32 us

profile of v3, /device:TPU:24, one launch (start us, length us, event | category | flops | bytes accessed | tf_op | source)
XLA Modules:
  0.0 58.2 jit_solution(3309619590521650442)
XLA Ops:
  0.0 56.9 %shard_map.37 = bf16[256,4096]{1,0:T(8,128)(2,1)S(1)} custom-call(bf16[256,4096]{1,0:T(8,128)(2,1)} %q_hbm.1, bf16[256,2048]{1,0:T(8,128)(2,1)} %k_hbm.1, bf16[256,2048]{1,0:T(8,128)(2,1)} %v_hbm.1), custom_call_target="tpu_custom_call" | custom-call | flops 5368709120 | bytes 16777216 | tf_op jit(solution)/shard_map/pallas_call | solution.py:271
  56.9 1.3 %copy.5 = bf16[256,4096]{1,0:T(8,128)(2,1)} copy(bf16[256,4096]{1,0:T(8,128)(2,1)S(1)} %shard_map.37) | data formatting | bytes 4194304
